TPU v7x, 32 devices: a whole 2x2x4 slice. The times are simulated.
32 devices in a mesh: chan: 4 (over y, x), head: 4 (over z), region: 2 (over core).
Axes of the slice: x: 2, y: 2, z: 4, core: 2. Of those that a mesh axis runs over, the one named last changes fastest.
Arguments:
- tokens: bfloat16 [64, 16, 4096], P('chan', 'region', 'head'), parts along dimension 1, may hold values from -56 to 56
- position: bfloat16 [64, 4096], P('chan', 'head'), may hold values from -3 to 3
- gain: bfloat16 [4096], P('head'), may hold values from 0.099609375 to 1.8984375
- qkv_weight: bfloat16 [3, 4096, 2048], P(None, 'chan', 'head'), may hold values from -0.09375 to 0.09375
- out_weight: bfloat16 [2048, 4096], P('head'), may hold values from -0.25 to 0.25
- cotangent: bfloat16 [64, 16, 4096], P('chan', 'region', 'head'), parts along dimension 1, may hold values from -6 to 6
Outputs:
- layer_out: bfloat16 [64, 16, 4096], P('chan', 'region', 'head'), parts along dimension 1
- input_grad: bfloat16 [64, 16, 4096], P('chan', 'region', 'head'), parts along dimension 1
There are 2 independent parts, one for each index of `region`. A program takes and returns all parts, laid end to end along the dimension named above; an argument that names none is the same for every part. Nothing has to cross between parts.
All inputs are finite; a program needn't handle non-finite values.
Results may differ from a plain program's by a relative error of at most 0.01.
Values may be sent and summed in bfloat16 or wider, within the bound.
A program may use at most 64 MiB of HBM per device.

v0:
```python
import jax
import jax.numpy as jnp
from jax import lax
from jax.sharding import PartitionSpec as P

HDIM = 128


def head_norm(values):
    return values * lax.rsqrt(jnp.mean(values * values, axis=-1, keepdims=True) + 1e-06)


def within_group(queries, keys_in, values):
    factor = queries.shape[-1] ** (-0.5)
    scores = jnp.einsum("cpne,dpne->pncd", head_norm(queries), head_norm(keys_in)) * factor
    weights = jnp.exp(scores)
    weights = weights / jnp.sum(weights, axis=-1, keepdims=True)
    return jnp.einsum("pncd,dpne->cpne", weights, values)


def across_groups(queries, aggregates):
    factor = queries.shape[-1] ** (-0.5)
    scores = jnp.einsum("cpne,gpne->cpng", head_norm(queries), head_norm(aggregates)) * factor
    weights = jnp.exp(scores)
    weights = weights / jnp.sum(weights, axis=-1, keepdims=True)
    return jnp.einsum("cpng,gpne->cpne", weights, aggregates)


def per_device(tokens, position, gain, qkv_weight, out_weight, cotangent):
    hidden_in = (tokens.astype(jnp.float32) + position[:, None, :].astype(jnp.float32)).astype(
        jnp.bfloat16
    )
    hidden_all, gain_all = (
        lax.all_gather(hidden_in, "head", axis=2, tiled=True),
        lax.all_gather(gain, "head", axis=0, tiled=True),
    )
    channels, patches, width = hidden_all.shape
    row_count = channels * patches
    hidden_f = hidden_all.astype(jnp.float32)
    inv_rms = lax.rsqrt(jnp.mean(hidden_f * hidden_f, axis=-1, keepdims=True) + 1e-05)
    gain_f = gain_all.astype(jnp.float32)
    normed = (hidden_f * inv_rms * gain_f).astype(jnp.bfloat16).reshape(row_count, width)
    weights_all = lax.all_gather(qkv_weight, "chan", axis=1, tiled=True)
    local_heads = weights_all.shape[2] // HDIM
    projected = jnp.einsum("td,jdf->jtf", normed, weights_all, preferred_element_type=jnp.float32)
    projected = lax.optimization_barrier(projected.astype(jnp.bfloat16)).astype(jnp.float32)
    shaped = projected.reshape(3, channels, patches, local_heads, HDIM)
    queries, keys_in, values = (shaped[0], shaped[1], shaped[2])
    first = within_group(queries, keys_in, values)
    group_mean = jnp.mean(first, axis=0, keepdims=True).astype(jnp.bfloat16)
    gathered_means = lax.all_gather(group_mean, "chan", axis=0, tiled=True)
    aggregates = gathered_means.astype(jnp.float32)
    second = across_groups(queries, aggregates)
    mixed = (first + second).astype(jnp.bfloat16).reshape(row_count, local_heads * HDIM)
    partial_out = jnp.dot(mixed, out_weight, preferred_element_type=jnp.float32).reshape(
        channels, patches, width
    )
    summed = lax.psum_scatter(partial_out, "head", scatter_dimension=2, tiled=True)
    layer_out = (summed + hidden_in.astype(jnp.float32)).astype(jnp.bfloat16)
    cotangent_all = lax.all_gather(cotangent, "head", axis=2, tiled=True)
    grad_mixed = lax.dot_general(
        cotangent_all.reshape(row_count, width),
        out_weight,
        (((1,), (1,)), ((), ())),
        preferred_element_type=jnp.float32,
    )
    grad_mixed = grad_mixed.reshape(channels, patches, local_heads, HDIM)
    unused_second, back_across = jax.vjp(across_groups, queries, aggregates)
    grad_q_second, grad_aggregates = back_across(grad_mixed)
    own_grad = lax.psum_scatter(grad_aggregates, "chan", scatter_dimension=0, tiled=True)
    grad_first = grad_mixed + own_grad / channels
    unused_first, back_within = jax.vjp(within_group, queries, keys_in, values)
    grad_q, grad_k, grad_v = back_within(grad_first)
    stacked = jnp.stack([grad_q + grad_q_second, grad_k, grad_v]).astype(jnp.bfloat16)
    stacked = stacked.reshape(3, row_count, local_heads * HDIM)
    grad_partial = jnp.einsum(
        "jtf,jdf->td", stacked, weights_all, preferred_element_type=jnp.float32
    )
    grad_partial = grad_partial.reshape(channels, patches, width)
    grad_share = lax.psum_scatter(grad_partial, "head", scatter_dimension=2, tiled=True)
    hidden_own = hidden_in.astype(jnp.float32)
    gain_own = gain.astype(jnp.float32)
    inner_dots = lax.psum(jnp.sum(hidden_own * gain_own * grad_share, axis=-1), "head")
    correction = inner_dots[..., None] / width
    grad_hidden = (
        inv_rms * gain_own * grad_share - hidden_own * inv_rms * inv_rms * inv_rms * correction
    )
    input_grad = (cotangent.astype(jnp.float32) + grad_hidden).astype(jnp.bfloat16)
    return (layer_out, input_grad)


def solution(mesh):
    return jax.shard_map(
        per_device,
        mesh=mesh,
        in_specs=(
            P("chan", "region", "head"),
            P("chan", "head"),
            P("head"),
            P(None, "chan", "head"),
            P("head", None),
            P("chan", "region", "head"),
        ),
        out_specs=(P("chan", "region", "head"), P("chan", "region", "head")),
        check_vma=False,
    )
```

profile of v0, /device:TPU:0, one launch (start us, length us, event | category | flops | bytes accessed | tf_op | source)
XLA Modules:
  0.0 347.8 jit_solution(13533118021965552499)
XLA Ops:
  7.2 0.8 convert_element_type.67
  8.0 1.7 add_convert_fusion
  9.8 0.7 all-gather.9.cloned.1.call-update
  10.5 0.7 all-gather.7.cloned.1.call-update
  11.3 13.7 %all_gather.16 = bf16[4096]{0:T(1024)(128)(2,1)S(1)} all-gather(bf16[1024]{0:T(1024)(128)(2,1)S(1)} %copy-done.3), channel_id=1, replica_groups=mesh['chan'=4,'head'=4,'region'=2] {'head'}, dimensions={0}, use_global_device_ids=true | all-gather | bytes 10240 | tf_op jit(solution)/shard_map/all_gather | solution.py:35
  24.9 15.9 %all-gather.5.cloned.1.call-done = bf16[16,8,4096]{2,1,0:T(8,128)(2,1)} async-done(((bf16[16,8,1024]{2,1,0:T(8,128)(2,1)}), bf16[16,8,4096]{2,1,0:T(8,128)(2,1)}) %all-gather.5.cloned.1.call-update) | async-done | bytes 1048592 | tf_op jit(solution)/shard_map/all_gather | solution.py:34
  40.9 1.5 fusion.7
  42.4 27.5 %all-gather.9.cloned.1.call-done = bf16[16,8,4096]{2,1,0:T(8,128)(2,1)} async-done(((bf16[16,8,1024]{2,1,0:T(8,128)(2,1)}), bf16[16,8,4096]{2,1,0:T(8,128)(2,1)}) %all-gather.9.cloned.1.call-update) | async-done | bytes 1048592 | tf_op jit(solution)/shard_map/all_gather | solution.py:60
  69.8 4.1 %convolution_bitcast_fusion.2 = f32[8,4,128,16]{2,0,1,3:T(8,128)S(1)} fusion(bf16[4,128,4096,1]{2,1,0,3:T(8,128)(2,1)} %bitcast.113, bf16[16,8,4096]{2,1,0:T(8,128)(2,1)} %all-gather.9.cloned.1.call-done), kind=kOutput, calls=%fused_computation.14 | convolution fusion | flops 536870912 | bytes 5505024 | tf_op jit(solution)/shard_map/dot_general | solution.py:61
  73.9 119.8 %all-gather.7.cloned.1.call-done = bf16[3,4096,512]{2,1,0:T(8,128)(2,1)} async-done(((bf16[3,1024,512]{2,1,0:T(8,128)(2,1)}), bf16[3,4096,512]{2,1,0:T(8,128)(2,1)}) %all-gather.7.cloned.1.call-update) | async-done | bytes 12582928 | tf_op jit(solution)/shard_map/all_gather | solution.py:43
  193.7 6.4 %fusion.10 = bf16[3,128,512]{2,1,0:T(8,128)(2,1)S(1)} fusion(bf16[3,4096,512]{2,1,0:T(8,128)(2,1)} %all-gather.7.cloned.1.call-done, bf16[16,8,4096]{2,1,0:T(8,128)(2,1)S(1)} %copy-done, f32[4096]{0:T(1024)S(1)} %convert_element_type.70, f32[16,8]{1,0:T(8,128)S(1)} %add_rsqrt_fusion), kind=kOutput, calls=%fused_computation.11 | convolution fusion | flops 1612906496 | bytes 14041600 | tf_op jit(solution)/shard_map/td,jdf->jtf/dot_general | solution.py:45
  200.8 0.5 fusion.80
  201.6 8.1 %all-gather = bf16[32,4,128]{2,1,0:T(4,128)(2,1)S(1)} all-gather(bf16[8,4,128]{2,1,0:T(4,128)(2,1)S(1)} %multiply_convert_fusion), channel_id=2, replica_groups=mesh['chan'=4,'head'=4,'region'=2] {'chan'}, dimensions={0}, use_global_device_ids=true | all-gather | bytes 40960 | tf_op jit(solution)/shard_map/all_gather | solution.py:51
  211.5 0.7 copy.128
  212.3 23.8 %reduce-scatter.10.cloned.1.call-done = f32[1,8,4,128]{3,1,2,0:T(8,128)} async-done(((f32[4,8,4,128]{3,1,2,0:T(8,128)}), f32[1,8,4,128]{3,1,2,0:T(8,128)}) %reduce-scatter.10.cloned.1.call-update) | async-done | bytes 16400
  236.1 0.7 multiply_bitcast_fusion
  237.8 0.6 multiply_reduce_fusion.2
  239.2 10.1 %fusion.2 = f32[16,8,4096]{2,1,0:T(8,128)} fusion(bf16[3,4096,512]{2,1,0:T(8,128)(2,1)} %all-gather.7.cloned.1.call-done, bf16[1,128,512]{2,1,0:T(8,128)(2,1)S(1)} %bitcast.114, bf16[1,128,512]{2,1,0:T(8,128)(2,1)S(1)} %bitcast.116, bf16[1,128,512]{2,1,0:T(8,128)(2,1)S(1)} %bitcast.115), kind=kOutput, calls=%fused_computation.2 | convolution fusion | flops 1611005952 | bytes 15073280 | tf_op jit(solution)/shard_map/jtf,jdf->td/dot_general | solution.py:76
  249.6 4.3 %fusion.5 = f32[16,8,4096]{2,1,0:T(8,128)} fusion(bf16[512,4096]{1,0:T(8,128)(2,1)} %param.10, bf16[16,8,4,128]{3,0,2,1:T(8,128)(2,1)S(1)} %fusion.13), kind=kOutput, calls=%fused_computation.3 | convolution fusion | flops 536870912 | bytes 6422528 | tf_op jit(solution)/shard_map/dot_general | solution.py:55
  254.0 39.3 %reduce-scatter.8.cloned.1.call-done = f32[16,8,1024]{2,1,0:T(8,128)} async-done(((f32[16,8,4096]{2,1,0:T(8,128)}), f32[16,8,1024]{2,1,0:T(8,128)}) %reduce-scatter.8.cloned.1.call-update) | async-done | bytes 524304 | tf_op jit(solution)/shard_map/reduce_scatter | solution.py:80
  293.3 1.2 fusion.32
  294.6 10.2 %psum.7 = f32[16,8]{1,0:T(8,128)S(1)} all-reduce(f32[16,8]{1,0:T(8,128)S(1)} %fusion.32), channel_id=1, replica_groups=mesh['chan'=4,'head'=4,'region'=2] {'head'}, use_global_device_ids=true, to_apply=%region_17.0 | all-reduce | flops 128 | bytes 1024 | tf_op jit(solution)/shard_map/psum | solution.py:83
  304.7 34.0 %reduce-scatter.6.cloned.1.call-done = f32[16,8,1024]{2,1,0:T(8,128)} async-done(((f32[16,8,4096]{2,1,0:T(8,128)}), f32[16,8,1024]{2,1,0:T(8,128)}) %reduce-scatter.6.cloned.1.call-update) | async-done | bytes 524304 | tf_op jit(solution)/shard_map/reduce_scatter | solution.py:58
  338.7 2.2 fusion.30
  (61 shorter events, 4.9 us)
Async XLA Ops:
  7.2 4.1 %copy-start.3 = (bf16[1024]{0:T(1024)(128)(2,1)S(1)}, bf16[1024]{0:T(1024)(128)(2,1)}, u32[]{:S(2)}) copy-start(bf16[1024]{0:T(1024)(128)(2,1)} %param.8) | copy-start | bytes 6148
  7.2 33.7 %all-gather.5.cloned.1.call-start = ((), (), s32[]{:S(2)}) async-start(), calls=%async_computation.3 | async-start | bytes 1310720 | tf_op jit(solution)/shard_map/all_gather | solution.py:34
  9.7 60.1 %all-gather.9.cloned.1.call-start = ((), (), s32[]{:S(2)}) async-start(), calls=%async_computation.6 | async-start | bytes 1310720 | tf_op jit(solution)/shard_map/all_gather | solution.py:60
  10.5 183.3 %all-gather.7.cloned.1.call-start = ((), (), s32[]{:S(2)}) async-start(), calls=%async_computation.4 | async-start | bytes 15728640 | tf_op jit(solution)/shard_map/all_gather | solution.py:43
  11.2 224.9 %reduce-scatter.10.cloned.1.call-start = ((), (), s32[]{:S(2)}) async-start(), calls=%async_computation.8 | async-start | bytes 81920
  69.8 123.9 %copy-start = (bf16[16,8,4096]{2,1,0:T(8,128)(2,1)S(1)}, bf16[16,8,4096]{2,1,0:T(8,128)(2,1)}, u32[]{:S(2)}) copy-start(bf16[16,8,4096]{2,1,0:T(8,128)(2,1)} %all-gather.5.cloned.1.call-done) | copy-start | bytes 3145732
  212.2 81.1 %reduce-scatter.8.cloned.1.call-start = ((), (), s32[]{:S(2)}) async-start(), calls=%async_computation.7 | async-start | bytes 2621440 | tf_op jit(solution)/shard_map/reduce_scatter | solution.py:80
  249.3 89.4 %reduce-scatter.6.cloned.1.call-start = ((), (), s32[]{:S(2)}) async-start(), calls=%async_computation.5 | async-start | bytes 2621440 | tf_op jit(solution)/shard_map/reduce_scatter | solution.py:58
  249.6 43.7 %copy-start.1 = (bf16[16,8,1024]{2,1,0:T(8,128)(2,1)S(1)}, bf16[16,8,1024]{2,1,0:T(8,128)(2,1)}, u32[]{:S(2)}) copy-start(bf16[16,8,1024]{2,1,0:T(8,128)(2,1)} %param.6) | copy-start | bytes 786436
  249.6 89.1 %copy-start.2 = (bf16[16,8,1024]{2,1,0:T(8,128)(2,1)S(1)}, bf16[16,8,1024]{2,1,0:T(8,128)(2,1)}, u32[]{:S(2)}) copy-start(bf16[16,8,1024]{2,1,0:T(8,128)(2,1)} %param.11) | copy-start | bytes 786436
Sparse Core Ops, SparseCore 0:
  10.2 30.6 all-gather.4
  42.4 27.3 all-gather.8
  71.7 122.0 all-gather.6
  212.3 23.6 reduce-scatter.9
  249.4 43.8 reduce-scatter.7
  295.5 43.1 reduce-scatter.5
where the time goes:
time: 348 us
  waiting for transfers between devices  262 us (75%)
  blocking collectives  31.9 us (9%)
  matrix products  29.1 us (8%)
  between operations  14.4 us (4%)
  other arithmetic  9.27 us (3%)
    all_gather x1, waiting for transfers between devices, per_device(): weights_all = lax.all_gather(qkv_weight, 'chan', axis=1, tiled=True)  120 us
    reduce_scatter x1, waiting for transfers between devices, per_device(): lax.psum_scatter(grad_partial, 'head', scatter_dimension=2, tiled=True)  39.3 us
    reduce_scatter x1, waiting for transfers between devices, per_device(): lax.psum_scatter(partial_out, 'head', scatter_dimension=2, tiled=True)  34 us
    all_gather x1, waiting for transfers between devices, per_device(): cotangent_all = lax.all_gather(cotangent, 'head', axis=2, tiled=True)  27.5 us
    unnamed x7, waiting for transfers between devices  25.2 us
    all_gather x1, waiting for transfers between devices, per_device(): lax.all_gather(hidden_in, 'head', axis=2, tiled=True)  15.9 us
    all_gather x1, blocking collectives, per_device(): lax.all_gather(gain, 'head', axis=0, tiled=True)  13.7 us
    psum x1, blocking collectives, per_device(): lax.psum(jnp.sum(hidden_own * gain_own * grad_share, axis=-1), 'head')  10.2 us
  transfers between devices with their start and end apart: 6, of which 6 were waited for; matrix products, arithmetic and copies ran while one was open for 3% of the time, Pallas kernels for 0%

commit v1 on v0

v1 whole, which is shorter than its diff:
```python
import functools

import jax
import jax.numpy as jnp
from jax import lax
from jax.experimental import pallas as pl
from jax.experimental.pallas import tpu as pltpu
from jax.sharding import PartitionSpec as P

HDIM = 128
MESH = pl.DeviceIdType.MESH
F32 = jnp.float32
BF16 = jnp.bfloat16

NN = (((1,), (0,)), ((), ()))
NT = (((1,), (1,)), ((), ()))
TN = (((0,), (0,)), ((), ()))


def mm(a, b, dims):
    return lax.dot_general(a, b, dims, preferred_element_type=F32)


def unit(u):
    r = lax.rsqrt(jnp.mean(u * u, axis=-1, keepdims=True) + 1e-06)
    return u * r, r


def unit_back(y, r, dy):
    return r * (dy - y * jnp.mean(y * dy, axis=-1, keepdims=True))


def same_patch(rows, columns, patches):
    a = lax.broadcasted_iota(jnp.int32, (rows, columns), 0)
    b = lax.broadcasted_iota(jnp.int32, (rows, columns), 1)
    return (a % patches == b % patches).astype(F32)


def softmax(a, b, mask):
    w = jnp.exp(mm(a.astype(BF16), b.astype(BF16), NT) * HDIM ** (-0.5)) * mask
    return w / jnp.sum(w, axis=-1, keepdims=True)


def kernel(
    C, H, R, patches,
    hid, cot, gain8, qkv, ow, lay_ref, inp_ref,
    wall, wo, hall, call, gall, normed, inv, proj, gm, wts, aggs, gq2, gsend, grecv,
    grads, s1, r1, s2, r2, own1, own2, corr, rcorr,
    loc, wsnd, wrcv, hs, hr, cs, cr, gs, gr, as_, ar, gas, gar, s1s, s1r, s2s, s2r, ks, kr,
):
    c, h, r = lax.axis_index("chan"), lax.axis_index("head"), lax.axis_index("region")
    T, W = hid.shape
    S, F = qkv.shape[1], qkv.shape[2]
    heads = F // HDIM
    chg = T // patches
    square = C == 4 and R == 2
    half = S // 2

    def remote(src, dst, ss, rs, **where):
        return pltpu.make_async_remote_copy(
            src_ref=src, dst_ref=dst, send_sem=ss, recv_sem=rs, device_id=where, device_id_type=MESH
        )

    barrier = pltpu.get_barrier_semaphore()
    for k in range(1, C):
        pl.semaphore_signal(barrier, inc=1, device_id={"chan": lax.rem(c + k, C)}, device_id_type=MESH)
    for k in range(1, H):
        pl.semaphore_signal(barrier, inc=1, device_id={"head": lax.rem(h + k, H)}, device_id_type=MESH)
    extra = 0
    if square:
        extra = 1
        pl.semaphore_signal(barrier, inc=1, device_id={"region": 1 - r}, device_id_type=MESH)

    own_w = pltpu.make_async_copy(qkv, wall.at[:, pl.ds(pl.multiple_of(c * S, S), S)], loc.at[0])
    own_w.start()
    own_o = []
    for i in range(H):
        cp = pltpu.make_async_copy(ow.at[:, pl.ds(i * W, W)], wo.at[i], loc.at[1 + i])
        cp.start()
        own_o.append(cp)
    pl.semaphore_wait(barrier, C - 1 + H - 1 + extra)

    sent = []

    def to_heads(src, buf, ss, rs):
        for k in range(1, H):
            cp = remote(src, buf.at[h], ss.at[k - 1], rs.at[k - 1], head=lax.rem(h + k, H))
            cp.start()
            sent.append(cp)

    def from_heads(buf, ss, rs):
        for k in range(1, H):
            slot = buf.at[lax.rem(h + H - k, H)]
            remote(slot, slot, ss.at[k - 1], rs.at[k - 1], head=lax.rem(h + k, H)).wait_recv()

    def rows_of(j, block, part):
        return wall.at[j, pl.ds(pl.multiple_of(block * S + part * half, half), half)]

    if square:
        y, x = c // 2, c % 2
        xn, yn, dg = y * 2 + 1 - x, (1 - y) * 2 + x, (1 - y) * 2 + 1 - x
        near = (xn * (1 - r) + yn * r, yn * (1 - r) + xn * r)
        mate_near = (near[1], near[0])
        blocks = (near[0], near[1], dg)
        mate_blocks = (mate_near[0], mate_near[1], dg)

        def put(slot, j, src, block, part, **where):
            i = slot * 3 + j
            cp = remote(src, rows_of(j, block, part), wsnd.at[i], wrcv.at[i], **where)
            cp.start()
            sent.append(cp)

        def took(slot, j):
            i = slot * 3 + j
            if slot < 3:
                ref = rows_of(j, blocks[slot], r)
            else:
                ref = rows_of(j, mate_blocks[slot - 3], 1 - r)
            remote(ref, ref, wsnd.at[i], wrcv.at[i], region=1 - r).wait_recv()

        def pass_on(slot, j):
            took(slot, j)
            src = rows_of(j, blocks[slot], r)
            if slot == 0:
                put(2, j, src, blocks[0], r, chan=near[1])
            put(3 + slot, j, src, blocks[slot], r, region=1 - r)

    to_heads(hid, hall, hs, hr)
    to_heads(gain8, gall, gs, gr)
    if square:
        for j in range(3):
            src = qkv.at[j, pl.ds(pl.multiple_of(r * half, half), half)]
            put(0, j, src, c, r, chan=near[0])
            put(1, j, src, c, r, chan=near[1])
    else:
        mine = pl.ds(pl.multiple_of(c * S, S), S)
        for k in range(1, C):
            cp = remote(qkv, wall.at[:, mine], wsnd.at[k - 1], wrcv.at[k - 1], chan=lax.rem(c + k, C))
            cp.start()
            sent.append(cp)
    to_heads(cot, call, cs, cr)
    hall[h] = hid[...]
    call[h] = cot[...]
    gall[h] = gain8[...]

    if square:
        pass_on(0, 0)
        pass_on(1, 0)

    from_heads(hall, hs, hr)
    from_heads(gall, gs, gr)
    total = jnp.zeros((T, 1), F32)
    for i in range(H):
        b = hall[i].astype(F32)
        total += jnp.sum(b * b, axis=-1, keepdims=True)
    scale = lax.rsqrt(total / (H * W) + 1e-05)
    inv[...] = jnp.broadcast_to(scale, inv.shape)

    def norm_block(i, carry):
        normed[i] = (hall[i].astype(F32) * inv[:, :1] * gall[i][:1, :]).astype(BF16)
        return carry

    lax.fori_loop(0, H, norm_block, 0)

    if square:
        for j in (1, 2):
            pass_on(0, j)
            pass_on(1, j)

    for cp in own_o:
        cp.wait()
    from_heads(call, cs, cr)
    gm[...] = jnp.zeros_like(gm)

    def mixed_block(i, carry):
        gm[...] += mm(call[i], wo[i], NT)
        return carry

    lax.fori_loop(0, H, mixed_block, 0)

    own_w.wait()
    if square:
        for j in range(3):
            pass_on(2, j)
    else:
        for k in range(1, C):
            ref = wall.at[:, pl.ds(pl.multiple_of(lax.rem(c + C - k, C) * S, S), S)]
            remote(ref, ref, wsnd.at[k - 1], wrcv.at[k - 1], chan=lax.rem(c + k, C)).wait_recv()
    for j in range(3):
        if square:
            for slot in (3, 4, 5):
                took(slot, j)
        own1[:, :F] = jnp.zeros((T, F), F32)

        def project(i, carry):
            own1[:, :F] += mm(normed[i], wall[j, pl.ds(pl.multiple_of(i * W, W), W), :], NN)
            return carry

        lax.fori_loop(0, H, project, 0)
        proj[j] = own1[:, :F].astype(BF16)

    mask = same_patch(T, T, patches)
    for n in range(heads):
        cols = slice(n * HDIM, (n + 1) * HDIM)
        qn, _ = unit(proj[0][:, cols].astype(F32))
        kn, _ = unit(proj[1][:, cols].astype(F32))
        w = softmax(qn, kn, mask)
        wts[n] = w
        first = mm(w.astype(BF16), proj[2][:, cols], NN)
        own2[:, cols] = first
        mean = jnp.mean(first.reshape(chg, patches, HDIM), axis=0)
        own1[:patches, cols] = mean.astype(BF16).astype(F32)
    aggs[c] = own1[:patches, :F]

    def to_groups(src_of, buf, ss, rs):
        for k in range(1, C):
            peer = lax.rem(c + k, C)
            cp = remote(src_of(peer), buf.at[c], ss.at[k - 1], rs.at[k - 1], chan=peer)
            cp.start()
            sent.append(cp)

    def from_groups(buf, ss, rs):
        for k in range(1, C):
            slot = buf.at[lax.rem(c + C - k, C)]
            remote(slot, slot, ss.at[k - 1], rs.at[k - 1], chan=lax.rem(c + k, C)).wait_recv()

    to_groups(lambda peer: aggs.at[c], aggs, as_, ar)
    from_groups(aggs, as_, ar)

    mask2 = same_patch(T, C * patches, patches)
    for n in range(heads):
        cols = slice(n * HDIM, (n + 1) * HDIM)
        a = aggs[:, :, cols].reshape(C * patches, HDIM)
        a16 = a.astype(BF16)
        qn, rq = unit(proj[0][:, cols].astype(F32))
        an, ra = unit(a)
        w = softmax(qn, an, mask2)
        w16 = w.astype(BF16)
        own2[:, cols] += mm(w16, a16, NN)
        g16 = gm[:, cols].astype(BF16)
        dw = mm(g16, a16, NT)
        ds = w * (dw - jnp.sum(w * dw, axis=-1, keepdims=True)) * HDIM ** (-0.5)
        ds16 = ds.astype(BF16)
        gq2[:, cols] = unit_back(qn, rq, mm(ds16, an.astype(BF16), NN))
        da = mm(w16, g16, TN) + unit_back(an, ra, mm(ds16, qn.astype(BF16), TN))
        gsend[:, :, cols] = da.reshape(C, patches, HDIM)
    to_groups(lambda peer: gsend.at[peer], grecv, gas, gar)
    grecv[c] = gsend[c]

    mixed = own2[:, :F].astype(BF16)
    for k in range(1, H):
        peer = lax.rem(h + k, H)
        s1[k - 1] = mm(mixed, wo[peer], NN).astype(BF16)
        cp = remote(s1.at[k - 1], r1.at[k - 1], s1s.at[k - 1], s1r.at[k - 1], head=peer)
        cp.start()
        sent.append(cp)
    own1[...] = mm(mixed, wo[h], NN)

    from_groups(grecv, gas, gar)
    back = grecv[0]
    for i in range(1, C):
        back = back + grecv[i]
    back = back / chg

    for n in range(heads):
        cols = slice(n * HDIM, (n + 1) * HDIM)
        lift = jnp.broadcast_to(back[None, :, cols], (chg, patches, HDIM)).reshape(T, HDIM)
        g16 = (gm[:, cols] + lift).astype(BF16)
        qn, rq = unit(proj[0][:, cols].astype(F32))
        kn, rk = unit(proj[1][:, cols].astype(F32))
        w = wts[n]
        dw = mm(g16, proj[2][:, cols], NT)
        ds = w * (dw - jnp.sum(w * dw, axis=-1, keepdims=True)) * HDIM ** (-0.5)
        ds16 = ds.astype(BF16)
        dq = unit_back(qn, rq, mm(ds16, kn.astype(BF16), NN)) + gq2[:, cols]
        dk = unit_back(kn, rk, mm(ds16, qn.astype(BF16), TN))
        grads[0, :, cols] = dq.astype(BF16)
        grads[1, :, cols] = dk.astype(BF16)
        grads[2, :, cols] = mm(w.astype(BF16), g16, TN).astype(BF16)

    dots = jnp.zeros((T, 1), F32)
    for k in list(range(1, H)) + [0]:
        peer = lax.rem(h + k, H)
        own2[...] = jnp.zeros_like(own2)

        def back_proj(j, carry):
            own2[...] += mm(grads[j], wall[j, pl.ds(pl.multiple_of(peer * W, W), W), :], NT)
            return carry

        lax.fori_loop(0, 3, back_proj, 0)
        if k:
            s2[k - 1] = own2[...].astype(BF16)
            cp = remote(s2.at[k - 1], r2.at[k - 1], s2s.at[k - 1], s2r.at[k - 1], head=peer)
            cp.start()
            sent.append(cp)
        dots += jnp.sum(hall[peer].astype(F32) * gall[peer][:1, :] * own2[...], axis=-1, keepdims=True)
    corr[...] = jnp.broadcast_to(dots, corr.shape)
    for k in range(1, H):
        cp = remote(corr, rcorr.at[k - 1], ks.at[k - 1], kr.at[k - 1], head=lax.rem(h + k, H))
        cp.start()
        sent.append(cp)

    def from_shares(buf, ss, rs, k):
        slot = buf.at[k - 1]
        remote(slot, slot, ss.at[k - 1], rs.at[k - 1], head=lax.rem(h + k, H)).wait_recv()

    for k in range(1, H):
        from_shares(r1, s1s, s1r, k)
        own1[...] += r1[k - 1].astype(F32)
    lay_ref[...] = (hid[...].astype(F32) + own1[...]).astype(BF16)
    for k in range(1, H):
        from_shares(r2, s2s, s2r, k)
        own2[...] += r2[k - 1].astype(F32)
    for k in range(1, H):
        from_shares(rcorr, ks, kr, k)
        corr_k = rcorr[k - 1]
        dots += corr_k[:, :1]
    ir = inv[:, :1]
    grad = ir * gain8[:1, :] * own2[...] - hid[...].astype(F32) * (ir * ir * ir * dots / (H * W))
    inp_ref[...] = (cot[...].astype(F32) + grad).astype(BF16)
    for cp in sent:
        cp.wait_send()


def per_device(C, H, R, tokens, position, gain, qkv_weight, out_weight, cotangent):
    channels, patches, W = tokens.shape
    T = channels * patches
    hidden = (tokens.astype(F32) + position[:, None, :].astype(F32)).astype(BF16).reshape(T, W)
    cot = cotangent.reshape(T, W)
    gain8 = jnp.broadcast_to(gain.astype(F32)[None, :], (8, W))
    S, F = qkv_weight.shape[1:]
    heads = F // HDIM
    D = S * C
    V = pltpu.VMEM
    dma = lambda n: pltpu.SemaphoreType.DMA((n,))
    nw = 18 if (C == 4 and R == 2) else C - 1
    z, g = H - 1, C - 1
    vm = pl.BlockSpec(memory_space=pltpu.VMEM)
    hbm = pl.BlockSpec(memory_space=pl.ANY)
    lay, inp = pl.pallas_call(
        functools.partial(kernel, C, H, R, patches),
        out_shape=[jax.ShapeDtypeStruct((T, W), BF16)] * 2,
        in_specs=[vm, vm, vm, hbm, hbm],
        out_specs=[vm, vm],
        scratch_shapes=[
            V((3, D, F), BF16), V((H, F, W), BF16), V((H, T, W), BF16), V((H, T, W), BF16),
            V((H, 8, W), F32), V((H, T, W), BF16), V((T, HDIM), F32), V((3, T, F), BF16),
            V((T, F), F32), V((heads, T, T), F32), V((C, patches, F), F32), V((T, F), F32),
            V((C, patches, F), F32), V((C, patches, F), F32), V((3, T, F), BF16),
            V((z, T, W), BF16), V((z, T, W), BF16), V((z, T, W), BF16), V((z, T, W), BF16),
            V((T, W), F32), V((T, W), F32), V((T, HDIM), F32), V((z, T, HDIM), F32),
            dma(1 + H), dma(nw), dma(nw), dma(z), dma(z), dma(z), dma(z), dma(z), dma(z),
            dma(g), dma(g), dma(g), dma(g), dma(z), dma(z), dma(z), dma(z), dma(z), dma(z),
        ],
        compiler_params=pltpu.CompilerParams(
            collective_id=0, has_side_effects=True, vmem_limit_bytes=50 * 1024 * 1024
        ),
    )(hidden, cot, gain8, qkv_weight, out_weight)
    return lay.reshape(channels, patches, W), inp.reshape(channels, patches, W)


def solution(mesh):
    C, H, R = (mesh.shape[a] for a in ("chan", "head", "region"))
    return jax.shard_map(
        functools.partial(per_device, C, H, R),
        mesh=mesh,
        in_specs=(
            P("chan", "region", "head"),
            P("chan", "head"),
            P("head"),
            P(None, "chan", "head"),
            P("head", None),
            P("chan", "region", "head"),
        ),
        out_specs=(P("chan", "region", "head"), P("chan", "region", "head")),
        check_vma=False,
    )
```

time: 348 us -> 127 us (0.36)
  waiting for transfers between devices: 262 us -> 0 us
  Pallas kernels: 0 us -> 121 us
  blocking collectives: 31.9 us -> 0 us
  matrix products: 29.1 us -> 0 us
  between operations: 14.4 us -> 0.66 us
  other arithmetic: 9.27 us -> 1.76 us
    all_gather x3 -> x0, waiting for transfers between devices: 163 us -> none  [the longest x1 120 us: per_device(): weights_all = lax.all_gather(qkv_weight, 'chan', axis=1, tiled=True)]
    pallas_call x0 -> x1, Pallas kernels: none -> 121 us  [per_device(): pl.pallas_call(functools.partial(kernel, C, H, R, patches), out_shape=[ja...]
    reduce_scatter x2 -> x0, waiting for transfers between devices: 73.3 us -> none  [the longest x1 39.3 us: per_device(): lax.psum_scatter(grad_partial, 'head', scatter_dimension=2, tiled=True)]
    dot_general x16 -> x0, matrix products: 29.1 us -> none  [the longest x1 10.1 us: per_device(): jnp.einsum('jtf,jdf->td', stacked, weights_all, preferred_element_type=jn...]
    unnamed x7 -> x0, waiting for transfers between devices: 25.2 us -> none
    all_gather x2 -> x0, blocking collectives: 21.8 us -> none  [the longest x1 13.7 us: per_device(): lax.all_gather(gain, 'head', axis=0, tiled=True)]
    psum x1 -> x0, blocking collectives: 10.2 us -> none  [per_device(): lax.psum(jnp.sum(hidden_own * gain_own * grad_share, axis=-1), 'head')]
    convert_element_type x7 -> x1, other arithmetic: 4.82 us -> 0.76 us  [per_device(): position[:, None, :].astype(F32)]
  transfers between devices with their start and end apart: 6 -> 0, of which waited for: 6 -> 0; matrix products, arithmetic and copies ran while one was open for 3% -> 0% of each run, Pallas kernels for 0% -> 0%
where the time goes in v1:
time: 127 us
  Pallas kernels  121 us (95%)
  local copies, waits for them, and re-layouts  3.04 us (2%)
  other arithmetic  1.76 us (1%)
    pallas_call x1, Pallas kernels, per_device(): pl.pallas_call(functools.partial(kernel, C, H, R, patches), out_shape=[ja...  121 us

profile of v1, /device:TPU:0, one launch (start us, length us, event | category | flops | bytes accessed | tf_op | source)
XLA Modules:
  0.0 126.5 jit_solution(9956269687318318563)
XLA Ops:
  0.6 0.7 broadcast_in_dim.2.gain8
  1.3 0.8 convert_element_type.14
  2.1 1.0 fusion.hid
  3.1 0.0 copy-start
  3.1 0.9 copy-done
  4.0 121.1 %shard_map.77 = (bf16[128,1024]{1,0:T(8,128)(2,1)S(1)}, bf16[128,1024]{1,0:T(8,128)(2,1)S(1)}) custom-call(bf16[128,1024]{1,0:T(8,128)(2,1)S(1)} %fusion.hid, bf16[128,1024]{1,0:T(8,128)(2,1)S(1)} %bitcast.5, f32[8,1024]{1,0:T(8,128)S(1)} %broadcast_in_dim.2.gain8, bf16[3,1024,512]{2,1,0:T(8,128)(2,1)} %qkv.1, bf16[512,4096]{1,0:T(8,128)(2,1)} %ow.1), custom_call_target="tpu_custom_call" | custom-call | tf_op jit(solution)/shard_map/pallas_call | solution.py:340
  125.1 0.7 copy.10
  125.8 0.7 copy.11
Async XLA Ops:
  3.1 1.0 copy-start

commit v2 on v1

v2 whole, which is shorter than its diff:
```python
import functools

import jax
import jax.numpy as jnp
from jax import lax
from jax.experimental import pallas as pl
from jax.experimental.pallas import tpu as pltpu
from jax.sharding import PartitionSpec as P

HDIM = 128
MESH = pl.DeviceIdType.MESH
F32 = jnp.float32
BF16 = jnp.bfloat16

NN = (((1,), (0,)), ((), ()))
NT = (((1,), (1,)), ((), ()))
TN = (((0,), (0,)), ((), ()))


def mm(a, b, dims):
    return lax.dot_general(a, b, dims, preferred_element_type=F32)


def unit(u):
    r = lax.rsqrt(jnp.mean(u * u, axis=-1, keepdims=True) + 1e-06)
    return u * r, r


def unit_back(y, r, dy):
    return r * (dy - y * jnp.mean(y * dy, axis=-1, keepdims=True))


def same_patch(rows, columns, patches):
    a = lax.broadcasted_iota(jnp.int32, (rows, columns), 0)
    b = lax.broadcasted_iota(jnp.int32, (rows, columns), 1)
    return (a % patches == b % patches).astype(F32)


def softmax(a, b, mask):
    w = jnp.exp(mm(a.astype(BF16), b.astype(BF16), NT) * HDIM ** (-0.5)) * mask
    return w / jnp.sum(w, axis=-1, keepdims=True)


def kernel(
    C, H, R, G,
    tok, pos, gain1, cot3, qkv, ow, lay_ref, inp_ref,
    hid, cot, gain8, acc, wall, wo, hall, call, gall, normed, inv, proj, gm, wts, aggs, gq2, gsend, grecv,
    grads, s1, r1, s2, r2, own1, own2, corr, rcorr,
    loc, wsnd, wrcv, hs, hr, cs, cr, gs, gr, as_, ar, gas, gar, s1s, s1r, s2s, s2r, ks, kr,
):
    c, h, r = lax.axis_index("chan"), lax.axis_index("head"), lax.axis_index("region")
    T, W = hid.shape
    patches = tok.shape[1]
    S, F = qkv.shape[1], qkv.shape[2]
    FG = F // G
    heads = FG // HDIM
    chg = T // patches
    square = C == 4 and R == 2
    half = S // 2

    def remote(src, dst, ss, rs, **where):
        return pltpu.make_async_remote_copy(
            src_ref=src, dst_ref=dst, send_sem=ss, recv_sem=rs, device_id=where, device_id_type=MESH
        )

    barrier = pltpu.get_barrier_semaphore()
    for k in range(1, C):
        pl.semaphore_signal(barrier, inc=1, device_id={"chan": lax.rem(c + k, C)}, device_id_type=MESH)
    for k in range(1, H):
        pl.semaphore_signal(barrier, inc=1, device_id={"head": lax.rem(h + k, H)}, device_id_type=MESH)
    extra = 0
    if square:
        extra = 1
        pl.semaphore_signal(barrier, inc=1, device_id={"region": 1 - r}, device_id_type=MESH)

    own_w = []
    for n in range(G):
        dst = wall.at[n, :, pl.ds(pl.multiple_of(c * S, S), S)]
        cp = pltpu.make_async_copy(qkv.at[:, :, pl.ds(n * FG, FG)], dst, loc.at[H + n])
        cp.start()
        own_w.append(cp)
    own_o = []
    for i in range(H):
        cp = pltpu.make_async_copy(ow.at[:, pl.ds(i * W, W)], wo.at[i], loc.at[i])
        cp.start()
        own_o.append(cp)
    pl.semaphore_wait(barrier, C - 1 + H - 1 + extra)

    sent = []

    def to_heads(src, buf, ss, rs):
        for k in range(1, H):
            cp = remote(src, buf.at[h], ss.at[k - 1], rs.at[k - 1], head=lax.rem(h + k, H))
            cp.start()
            sent.append(cp)

    def from_heads(buf, ss, rs):
        for k in range(1, H):
            slot = buf.at[lax.rem(h + H - k, H)]
            remote(slot, slot, ss.at[k - 1], rs.at[k - 1], head=lax.rem(h + k, H)).wait_recv()

    def rows_of(n, block, part):
        return wall.at[n, :, pl.ds(pl.multiple_of(block * S + part * half, half), half)]

    if square:
        y, x = c // 2, c % 2
        xn, yn, dg = y * 2 + 1 - x, (1 - y) * 2 + x, (1 - y) * 2 + 1 - x
        near = (xn * (1 - r) + yn * r, yn * (1 - r) + xn * r)
        mate_near = (near[1], near[0])
        blocks = (near[0], near[1], dg)
        mate_blocks = (mate_near[0], mate_near[1], dg)

        def put(slot, j, src, block, part, **where):
            i = slot * G + j
            cp = remote(src, rows_of(j, block, part), wsnd.at[i], wrcv.at[i], **where)
            cp.start()
            sent.append(cp)

        def took(slot, j):
            i = slot * G + j
            if slot < 3:
                ref = rows_of(j, blocks[slot], r)
            else:
                ref = rows_of(j, mate_blocks[slot - 3], 1 - r)
            remote(ref, ref, wsnd.at[i], wrcv.at[i], region=1 - r).wait_recv()

        def pass_on(slot, j):
            took(slot, j)
            src = rows_of(j, blocks[slot], r)
            if slot == 0:
                put(2, j, src, blocks[0], r, chan=near[1])
            put(3 + slot, j, src, blocks[slot], r, region=1 - r)

    if square:
        for n in range(G):
            src = qkv.at[:, pl.ds(pl.multiple_of(r * half, half), half), pl.ds(n * FG, FG)]
            put(0, n, src, c, r, chan=near[0])
            put(1, n, src, c, r, chan=near[1])
    else:
        for n in range(G):
            for k in range(1, C):
                i = n * (C - 1) + k - 1
                src = qkv.at[:, :, pl.ds(n * FG, FG)]
                dst = wall.at[n, :, pl.ds(pl.multiple_of(c * S, S), S)]
                cp = remote(src, dst, wsnd.at[i], wrcv.at[i], chan=lax.rem(c + k, C))
                cp.start()
                sent.append(cp)
    hidden = (tok[...].astype(F32) + pos[...].astype(F32)[:, None, :]).astype(BF16)
    hid[...] = hidden.reshape(T, W)
    gain8[...] = jnp.broadcast_to(gain1[...].astype(F32), gain8.shape)
    to_heads(hid, hall, hs, hr)
    to_heads(gain8, gall, gs, gr)
    cot[...] = cot3[...].reshape(T, W)
    to_heads(cot, call, cs, cr)
    hall[h] = hid[...]
    call[h] = cot[...]
    gall[h] = gain8[...]

    if square:
        pass_on(0, 0)
        pass_on(1, 0)

    from_heads(hall, hs, hr)
    from_heads(gall, gs, gr)
    total = jnp.zeros((T, 1), F32)
    for i in range(H):
        b = hall[i].astype(F32)
        total += jnp.sum(b * b, axis=-1, keepdims=True)
    scale = lax.rsqrt(total / (H * W) + 1e-05)
    inv[...] = jnp.broadcast_to(scale, inv.shape)

    def norm_block(i, carry):
        normed[i] = (hall[i].astype(F32) * inv[:, :1] * gall[i][:1, :]).astype(BF16)
        return carry

    lax.fori_loop(0, H, norm_block, 0)

    def weights(n):
        own_w[n].wait()
        if square:
            pass_on(2, n)
            for slot in (3, 4, 5):
                took(slot, n)
        else:
            for k in range(1, C):
                ref = wall.at[n, :, pl.ds(pl.multiple_of(lax.rem(c + C - k, C) * S, S), S)]
                i = n * (C - 1) + k - 1
                remote(ref, ref, wsnd.at[i], wrcv.at[i], chan=lax.rem(c + k, C)).wait_recv()

    def to_groups(n, src_of, buf, ss, rs):
        for k in range(1, C):
            peer = lax.rem(c + k, C)
            i = n * (C - 1) + k - 1
            cp = remote(src_of(peer), buf.at[n, c], ss.at[i], rs.at[i], chan=peer)
            cp.start()
            sent.append(cp)

    def from_groups(n, buf, ss, rs):
        for k in range(1, C):
            slot = buf.at[n, lax.rem(c + C - k, C)]
            i = n * (C - 1) + k - 1
            remote(slot, slot, ss.at[i], rs.at[i], chan=lax.rem(c + k, C)).wait_recv()

    mask = same_patch(T, T, patches)
    mask2 = same_patch(T, C * patches, patches)

    def forward(n):
        own1[:, : 3 * FG] = jnp.zeros((T, 3 * FG), F32)

        def project(i, carry):
            rows = pl.ds(pl.multiple_of(i * W, W), W)
            for j in range(3):
                own1[:, j * FG : (j + 1) * FG] += mm(normed[i], wall[n, j, rows, :], NN)
            return carry

        lax.fori_loop(0, H, project, 0)
        for j in range(3):
            proj[n, j] = own1[:, j * FG : (j + 1) * FG].astype(BF16)
        for e in range(heads):
            cols = slice(e * HDIM, (e + 1) * HDIM)
            whole = slice(n * FG + e * HDIM, n * FG + (e + 1) * HDIM)
            qn, _ = unit(proj[n, 0][:, cols].astype(F32))
            kn, _ = unit(proj[n, 1][:, cols].astype(F32))
            w = softmax(qn, kn, mask)
            wts[n, e] = w
            first = mm(w.astype(BF16), proj[n, 2][:, cols], NN)
            own2[:, whole] = first
            mean = jnp.mean(first.reshape(chg, patches, HDIM), axis=0)
            own1[:patches, cols] = mean.astype(BF16).astype(F32)
        aggs[n, c] = own1[:patches, :FG]
        to_groups(n, lambda peer: aggs.at[n, c], aggs, as_, ar)

    def across(n):
        from_groups(n, aggs, as_, ar)
        for e in range(heads):
            cols = slice(e * HDIM, (e + 1) * HDIM)
            whole = slice(n * FG + e * HDIM, n * FG + (e + 1) * HDIM)
            a = aggs[n][:, :, cols].reshape(C * patches, HDIM)
            a16 = a.astype(BF16)
            qn, rq = unit(proj[n, 0][:, cols].astype(F32))
            an, ra = unit(a)
            w = softmax(qn, an, mask2)
            w16 = w.astype(BF16)
            own2[:, whole] += mm(w16, a16, NN)
            g16 = gm[:, whole].astype(BF16)
            dw = mm(g16, a16, NT)
            ds = w * (dw - jnp.sum(w * dw, axis=-1, keepdims=True)) * HDIM ** (-0.5)
            ds16 = ds.astype(BF16)
            gq2[:, whole] = unit_back(qn, rq, mm(ds16, an.astype(BF16), NN))
            da = mm(w16, g16, TN) + unit_back(an, ra, mm(ds16, qn.astype(BF16), TN))
            gsend[n, :, :, cols] = da.reshape(C, patches, HDIM)
        to_groups(n, lambda peer: gsend.at[n, peer], grecv, gas, gar)
        grecv[n, c] = gsend[n, c]

    def within(n):
        from_groups(n, grecv, gas, gar)
        back = grecv[n, 0]
        for i in range(1, C):
            back = back + grecv[n, i]
        back = back / chg
        for e in range(heads):
            cols = slice(e * HDIM, (e + 1) * HDIM)
            whole = slice(n * FG + e * HDIM, n * FG + (e + 1) * HDIM)
            lift = jnp.broadcast_to(back[None, :, cols], (chg, patches, HDIM)).reshape(T, HDIM)
            g16 = (gm[:, whole] + lift).astype(BF16)
            qn, rq = unit(proj[n, 0][:, cols].astype(F32))
            kn, rk = unit(proj[n, 1][:, cols].astype(F32))
            w = wts[n, e]
            dw = mm(g16, proj[n, 2][:, cols], NT)
            ds = w * (dw - jnp.sum(w * dw, axis=-1, keepdims=True)) * HDIM ** (-0.5)
            ds16 = ds.astype(BF16)
            dq = unit_back(qn, rq, mm(ds16, kn.astype(BF16), NN)) + gq2[:, whole]
            dk = unit_back(kn, rk, mm(ds16, qn.astype(BF16), TN))
            grads[0, :, cols] = dq.astype(BF16)
            grads[1, :, cols] = dk.astype(BF16)
            grads[2, :, cols] = mm(w.astype(BF16), g16, TN).astype(BF16)

    def back_proj(n, block):
        rows = pl.ds(pl.multiple_of(block * W, W), W)
        total = mm(grads[0], wall[n, 0, rows, :], NT)
        total += mm(grads[1], wall[n, 1, rows, :], NT)
        return total + mm(grads[2], wall[n, 2, rows, :], NT)

    if square:
        for n in range(1, G):
            pass_on(0, n)
            pass_on(1, n)
    for n in range(G):
        weights(n)
        forward(n)
        if n == 0:
            for cp in own_o:
                cp.wait()
            from_heads(call, cs, cr)
            gm[...] = jnp.zeros_like(gm)

            def mixed_block(i, carry):
                gm[...] += mm(call[i], wo[i], NT)
                return carry

            lax.fori_loop(0, H, mixed_block, 0)
        across(n)
        if n < G - 1:
            within(n)

            def add_block(i, carry):
                part = back_proj(n, i)
                acc[i] = part if n == 0 else acc[i] + part
                return carry

            lax.fori_loop(0, H, add_block, 0)

    mixed = own2[:, :F].astype(BF16)
    for k in range(1, H):
        peer = lax.rem(h + k, H)
        s1[k - 1] = mm(mixed, wo[peer], NN).astype(BF16)
        cp = remote(s1.at[k - 1], r1.at[k - 1], s1s.at[k - 1], s1r.at[k - 1], head=peer)
        cp.start()
        sent.append(cp)
    own1[...] = mm(mixed, wo[h], NN)

    within(G - 1)

    dots = jnp.zeros((T, 1), F32)
    for k in list(range(1, H)) + [0]:
        peer = lax.rem(h + k, H)
        part = back_proj(G - 1, peer)
        own2[...] = part if G == 1 else acc[peer] + part
        if k:
            s2[k - 1] = own2[...].astype(BF16)
            cp = remote(s2.at[k - 1], r2.at[k - 1], s2s.at[k - 1], s2r.at[k - 1], head=peer)
            cp.start()
            sent.append(cp)
        dots += jnp.sum(hall[peer].astype(F32) * gall[peer][:1, :] * own2[...], axis=-1, keepdims=True)
    corr[...] = jnp.broadcast_to(dots, corr.shape)
    for k in range(1, H):
        cp = remote(corr, rcorr.at[k - 1], ks.at[k - 1], kr.at[k - 1], head=lax.rem(h + k, H))
        cp.start()
        sent.append(cp)

    def from_shares(buf, ss, rs, k):
        slot = buf.at[k - 1]
        remote(slot, slot, ss.at[k - 1], rs.at[k - 1], head=lax.rem(h + k, H)).wait_recv()

    for k in range(1, H):
        from_shares(r1, s1s, s1r, k)
        own1[...] += r1[k - 1].astype(F32)
    lay_ref[...] = (hid[...].astype(F32) + own1[...]).astype(BF16).reshape(lay_ref.shape)
    for k in range(1, H):
        from_shares(r2, s2s, s2r, k)
        own2[...] += r2[k - 1].astype(F32)
    for k in range(1, H):
        from_shares(rcorr, ks, kr, k)
        corr_k = rcorr[k - 1]
        dots += corr_k[:, :1]
    ir = inv[:, :1]
    grad = ir * gain8[:1, :] * own2[...] - hid[...].astype(F32) * (ir * ir * ir * dots / (H * W))
    inp_ref[...] = (cot[...].astype(F32) + grad).astype(BF16).reshape(inp_ref.shape)
    for cp in sent:
        cp.wait_send()


def per_device(C, H, R, tokens, position, gain, qkv_weight, out_weight, cotangent):
    channels, patches, W = tokens.shape
    T = channels * patches
    S, F = qkv_weight.shape[1:]
    G = 2 if F % (4 * HDIM) == 0 else 1
    FG = F // G
    heads = FG // HDIM
    D = S * C
    V = pltpu.VMEM
    dma = lambda n: pltpu.SemaphoreType.DMA((n,))
    nw = 6 * G if (C == 4 and R == 2) else G * (C - 1)
    z, g = H - 1, G * (C - 1)
    vm = pl.BlockSpec(memory_space=pltpu.VMEM)
    hbm = pl.BlockSpec(memory_space=pl.ANY)
    return pl.pallas_call(
        functools.partial(kernel, C, H, R, G),
        out_shape=[jax.ShapeDtypeStruct(tokens.shape, BF16)] * 2,
        in_specs=[vm, vm, vm, vm, hbm, hbm],
        out_specs=[vm, vm],
        scratch_shapes=[
            V((T, W), BF16), V((T, W), BF16), V((8, W), F32), V((H, T, W), F32),
            V((G, 3, D, FG), BF16), V((H, F, W), BF16), V((H, T, W), BF16), V((H, T, W), BF16),
            V((H, 8, W), F32), V((H, T, W), BF16), V((T, HDIM), F32), V((G, 3, T, FG), BF16),
            V((T, F), F32), V((G, heads, T, T), F32), V((G, C, patches, FG), F32), V((T, F), F32),
            V((G, C, patches, FG), F32), V((G, C, patches, FG), F32), V((3, T, FG), BF16),
            V((z, T, W), BF16), V((z, T, W), BF16), V((z, T, W), BF16), V((z, T, W), BF16),
            V((T, W), F32), V((T, W), F32), V((T, HDIM), F32), V((z, T, HDIM), F32),
            dma(G + H), dma(nw), dma(nw), dma(z), dma(z), dma(z), dma(z), dma(z), dma(z),
            dma(g), dma(g), dma(g), dma(g), dma(z), dma(z), dma(z), dma(z), dma(z), dma(z),
        ],
        compiler_params=pltpu.CompilerParams(
            collective_id=0, has_side_effects=True, vmem_limit_bytes=50 * 1024 * 1024
        ),
    )(tokens, position, gain[None, :], cotangent, qkv_weight, out_weight)


def solution(mesh):
    C, H, R = (mesh.shape[a] for a in ("chan", "head", "region"))
    return jax.shard_map(
        functools.partial(per_device, C, H, R),
        mesh=mesh,
        in_specs=(
            P("chan", "region", "head"),
            P("chan", "head"),
            P("head"),
            P(None, "chan", "head"),
            P("head", None),
            P("chan", "region", "head"),
        ),
        out_specs=(P("chan", "region", "head"), P("chan", "region", "head")),
        check_vma=False,
    )
```

time: 127 us -> 133 us (1.047)
  Pallas kernels: 121 us -> 127 us
  other arithmetic: 1.76 us -> 0 us
  local copies, waits for them, and re-layouts: 3.04 us -> 4.75 us
    pallas_call x1, Pallas kernels: 121 us -> 127 us  [per_device(): pl.pallas_call(functools.partial(kernel, C, H, R, G), out_shape=[jax.Shap...]
    unnamed x4 -> x8, local copies, waits for them, and re-layouts: 2.35 us -> 4.06 us
where the time goes in v2:
time: 133 us; the launch traced here: 132 us
  Pallas kernels  127 us (95%)
  local copies, waits for them, and re-layouts  4.75 us (4%)
    pallas_call x1, Pallas kernels, per_device(): pl.pallas_call(functools.partial(kernel, C, H, R, G), out_shape=[jax.Shap...  127 us
    unnamed x8, local copies, waits for them, and re-layouts  4.06 us

profile of v2, /device:TPU:0, one launch (start us, length us, event | category | flops | bytes accessed | tf_op | source)
XLA Modules:
  0.0 132.3 jit_solution(16600700275058736053)
XLA Ops:
  0.6 0.7 broadcast_in_dim.3.gain1
  1.3 0.0 copy-start
  1.3 0.9 copy-done
  2.3 0.0 copy-start.1
  2.3 0.9 copy-done.1
  3.2 0.0 copy-start.2
  3.2 0.8 copy-done.2
  4.0 126.9 %shard_map.77 = (bf16[16,8,1024]{2,1,0:T(8,128)(2,1)S(1)}, bf16[16,8,1024]{2,1,0:T(8,128)(2,1)S(1)}) custom-call(bf16[16,8,1024]{2,1,0:T(8,128)(2,1)S(1)} %copy-done, bf16[16,1024]{1,0:T(8,128)(2,1)S(1)} %copy-done.2, bf16[1,1024]{1,0:T(2,128)(2,1)S(1)} %broadcast_in_dim.3.gain1, bf16[16,8,1024]{2,1,0:T(8,128)(2,1)S(1)} %copy-done.1, ...), custom_call_target="tpu_custom_call" | custom-call | tf_op jit(solution)/shard_map/pallas_call | solution.py:377
  130.9 0.7 copy.10
  131.6 0.7 copy.11
Async XLA Ops:
  1.3 0.9 copy-start
  2.3 0.9 copy-start.1
  3.2 0.8 copy-start.2

commit v3 on v2

--- a/solution.py
+++ b/solution.py
@@ -44,7 +44,7 @@
 def kernel(
     C, H, R, G,
     tok, pos, gain1, cot3, qkv, ow, lay_ref, inp_ref,
-    hid, cot, gain8, acc, wall, wo, hall, call, gall, normed, inv, proj, gm, wts, aggs, gq2, gsend, grecv,
+    hid, cot, gain8, acc, acc2, wall, wo, hall, call, gall, normed, inv, proj, gm, wts, aggs, gq2, gsend, grecv,
     grads, s1, r1, s2, r2, own1, own2, corr, rcorr,
     loc, wsnd, wrcv, hs, hr, cs, cr, gs, gr, as_, ar, gas, gar, s1s, s1r, s2s, s2r, ks, kr,
 ):
@@ -99,8 +99,8 @@
             slot = buf.at[lax.rem(h + H - k, H)]
             remote(slot, slot, ss.at[k - 1], rs.at[k - 1], head=lax.rem(h + k, H)).wait_recv()
 
-    def rows_of(n, block, part):
-        return wall.at[n, :, pl.ds(pl.multiple_of(block * S + part * half, half), half)]
+    def rows_of(j, block, part):
+        return wall.at[0, j, pl.ds(pl.multiple_of(block * S + part * half, half), half)]
 
     if square:
         y, x = c // 2, c % 2
@@ -111,13 +111,13 @@
         mate_blocks = (mate_near[0], mate_near[1], dg)
 
         def put(slot, j, src, block, part, **where):
-            i = slot * G + j
+            i = slot * 3 + j
             cp = remote(src, rows_of(j, block, part), wsnd.at[i], wrcv.at[i], **where)
             cp.start()
             sent.append(cp)
 
         def took(slot, j):
-            i = slot * G + j
+            i = slot * 3 + j
             if slot < 3:
                 ref = rows_of(j, blocks[slot], r)
             else:
@@ -132,10 +132,10 @@
             put(3 + slot, j, src, blocks[slot], r, region=1 - r)
 
     if square:
-        for n in range(G):
-            src = qkv.at[:, pl.ds(pl.multiple_of(r * half, half), half), pl.ds(n * FG, FG)]
-            put(0, n, src, c, r, chan=near[0])
-            put(1, n, src, c, r, chan=near[1])
+        for j in range(3):
+            src = qkv.at[j, pl.ds(pl.multiple_of(r * half, half), half)]
+            put(0, j, src, c, r, chan=near[0])
+            put(1, j, src, c, r, chan=near[1])
     else:
         for n in range(G):
             for k in range(1, C):
@@ -178,9 +178,8 @@
     def weights(n):
         own_w[n].wait()
         if square:
-            pass_on(2, n)
-            for slot in (3, 4, 5):
-                took(slot, n)
+            for j in range(3):
+                pass_on(2, j)
         else:
             for k in range(1, C):
                 ref = wall.at[n, :, pl.ds(pl.multiple_of(lax.rem(c + C - k, C) * S, S), S)]
@@ -205,17 +204,19 @@
     mask2 = same_patch(T, C * patches, patches)
 
     def forward(n):
-        own1[:, : 3 * FG] = jnp.zeros((T, 3 * FG), F32)
-
-        def project(i, carry):
-            rows = pl.ds(pl.multiple_of(i * W, W), W)
-            for j in range(3):
-                own1[:, j * FG : (j + 1) * FG] += mm(normed[i], wall[n, j, rows, :], NN)
-            return carry
-
-        lax.fori_loop(0, H, project, 0)
         for j in range(3):
-            proj[n, j] = own1[:, j * FG : (j + 1) * FG].astype(BF16)
+            if square:
+                for slot in (3, 4, 5):
+                    took(slot, j)
+            own1[:, :FG] = jnp.zeros((T, FG), F32)
+
+            def project(i, carry):
+                rows = pl.ds(pl.multiple_of(i * W, W), W)
+                own1[:, :FG] += mm(normed[i], wall[n, j, rows, :], NN)
+                return carry
+
+            lax.fori_loop(0, H, project, 0)
+            proj[n, j] = own1[:, :FG].astype(BF16)
         for e in range(heads):
             cols = slice(e * HDIM, (e + 1) * HDIM)
             whole = slice(n * FG + e * HDIM, n * FG + (e + 1) * HDIM)
@@ -282,95 +283,129 @@
         return total + mm(grads[2], wall[n, 2, rows, :], NT)
 
     if square:
-        for n in range(1, G):
-            pass_on(0, n)
-            pass_on(1, n)
-    for n in range(G):
-        weights(n)
-        forward(n)
-        if n == 0:
-            for cp in own_o:
-                cp.wait()
-            from_heads(call, cs, cr)
-            gm[...] = jnp.zeros_like(gm)
-
-            def mixed_block(i, carry):
-                gm[...] += mm(call[i], wo[i], NT)
-                return carry
-
-            lax.fori_loop(0, H, mixed_block, 0)
-        across(n)
-        if n < G - 1:
-            within(n)
-
-            def add_block(i, carry):
-                part = back_proj(n, i)
-                acc[i] = part if n == 0 else acc[i] + part
-                return carry
-
-            lax.fori_loop(0, H, add_block, 0)
-
+        pass_on(0, 1)
+        pass_on(1, 1)
+    for cp in own_o:
+        cp.wait()
+    from_heads(call, cs, cr)
+    gm[...] = jnp.zeros_like(gm)
+
+    def mixed_block(i, carry):
+        gm[...] += mm(call[i], wo[i], NT)
+        return carry
+
+    if square:
+        pass_on(0, 2)
+        pass_on(1, 2)
+    lax.fori_loop(0, H, mixed_block, 0)
+    weights(0)
+    forward(0)
+    across(0)
+
+    later = []
+
+    def chain_copy(way, m, snd, rcv, ss, rs):
+        i = way * (H - 1) + m
+        peer = lax.rem(h + 1, H) if way == 0 else lax.rem(h + H - 1, H)
+        return remote(snd.at[i], rcv.at[i], ss.at[i], rs.at[i], head=peer)
+
+    def chain_step(m, share, snd, rcv, ss, rs):
+        for way in range(2):
+            d = H - 1 - m if way == 0 else m
+            first = (h == 0) if way == 0 else (h == H - 1)
+            sends = (h < d) if way == 0 else (h > d)
+            i = way * (H - 1) + m
+            cp = chain_copy(way, m, snd, rcv, ss, rs)
+
+            @pl.when(jnp.logical_and(sends, jnp.logical_not(first)))
+            def _():
+                cp.wait_recv()
+                snd[i] = (share[d] + rcv[i].astype(F32)).astype(BF16)
+                cp.start()
+
+            later.append((sends, cp))
+
+    def chain_open(d, share, snd, rcv, ss, rs):
+        for way in range(2):
+            m = H - 1 - d if way == 0 else d
+            if m > H - 2:
+                continue
+            i = way * (H - 1) + m
+            first = (h == 0) if way == 0 else (h == H - 1)
+
+            @pl.when(first)
+            def _():
+                snd[i] = share[d].astype(BF16)
+                chain_copy(way, m, snd, rcv, ss, rs).start()
+
+    def chain_end(share, snd, rcv, ss, rs, total):
+        total[...] = share[h]
+        for way in range(2):
+            for m in range(H - 1):
+                d = H - 1 - m if way == 0 else m
+                i = way * (H - 1) + m
+
+                @pl.when(h == d)
+                def _():
+                    chain_copy(way, m, snd, rcv, ss, rs).wait_recv()
+                    total[...] += rcv[i].astype(F32)
+
+    order = []
+    for m in range((H + 1) // 2):
+        order += [H - 1 - m] + ([m] if m != H - 1 - m else [])
     mixed = own2[:, :F].astype(BF16)
-    for k in range(1, H):
-        peer = lax.rem(h + k, H)
-        s1[k - 1] = mm(mixed, wo[peer], NN).astype(BF16)
-        cp = remote(s1.at[k - 1], r1.at[k - 1], s1s.at[k - 1], s1r.at[k - 1], head=peer)
-        cp.start()
-        sent.append(cp)
-    own1[...] = mm(mixed, wo[h], NN)
-
-    within(G - 1)
+    one = (acc, s1, r1, s1s, s1r)
+    two = (acc2, s2, r2, s2s, s2r)
+    for d in order:
+        acc[d] = mm(mixed, wo[d], NN)
+        chain_open(d, *one)
+    chain_step(0, *one)
+    within(0)
+    for m in range(1, H - 2):
+        chain_step(m, *one)
 
     dots = jnp.zeros((T, 1), F32)
-    for k in list(range(1, H)) + [0]:
-        peer = lax.rem(h + k, H)
-        part = back_proj(G - 1, peer)
-        own2[...] = part if G == 1 else acc[peer] + part
-        if k:
-            s2[k - 1] = own2[...].astype(BF16)
-            cp = remote(s2.at[k - 1], r2.at[k - 1], s2s.at[k - 1], s2r.at[k - 1], head=peer)
-            cp.start()
-            sent.append(cp)
-        dots += jnp.sum(hall[peer].astype(F32) * gall[peer][:1, :] * own2[...], axis=-1, keepdims=True)
+    for d in order:
+        part = back_proj(0, d)
+        acc2[d] = part
+        chain_open(d, *two)
+        dots += jnp.sum(hall[d].astype(F32) * gall[d][:1, :] * part, axis=-1, keepdims=True)
+    for m in range(max(1, H - 2), H - 1):
+        chain_step(m, *one)
     corr[...] = jnp.broadcast_to(dots, corr.shape)
     for k in range(1, H):
         cp = remote(corr, rcorr.at[k - 1], ks.at[k - 1], kr.at[k - 1], head=lax.rem(h + k, H))
         cp.start()
         sent.append(cp)
-
-    def from_shares(buf, ss, rs, k):
-        slot = buf.at[k - 1]
-        remote(slot, slot, ss.at[k - 1], rs.at[k - 1], head=lax.rem(h + k, H)).wait_recv()
-
-    for k in range(1, H):
-        from_shares(r1, s1s, s1r, k)
-        own1[...] += r1[k - 1].astype(F32)
+    for m in range(H - 1):
+        chain_step(m, *two)
+    chain_end(*one, own1)
     lay_ref[...] = (hid[...].astype(F32) + own1[...]).astype(BF16).reshape(lay_ref.shape)
     for k in range(1, H):
-        from_shares(r2, s2s, s2r, k)
-        own2[...] += r2[k - 1].astype(F32)
-    for k in range(1, H):
-        from_shares(rcorr, ks, kr, k)
+        remote(rcorr.at[k - 1], rcorr.at[k - 1], ks.at[k - 1], kr.at[k - 1], head=lax.rem(h + k, H)).wait_recv()
         corr_k = rcorr[k - 1]
         dots += corr_k[:, :1]
+    chain_end(*two, own2)
     ir = inv[:, :1]
     grad = ir * gain8[:1, :] * own2[...] - hid[...].astype(F32) * (ir * ir * ir * dots / (H * W))
     inp_ref[...] = (cot[...].astype(F32) + grad).astype(BF16).reshape(inp_ref.shape)
     for cp in sent:
         cp.wait_send()
+    for sends, cp in later:
+        pl.when(sends)(cp.wait_send)
 
 
 def per_device(C, H, R, tokens, position, gain, qkv_weight, out_weight, cotangent):
     channels, patches, W = tokens.shape
     T = channels * patches
     S, F = qkv_weight.shape[1:]
-    G = 2 if F % (4 * HDIM) == 0 else 1
+    G = 1
     FG = F // G
     heads = FG // HDIM
     D = S * C
     V = pltpu.VMEM
     dma = lambda n: pltpu.SemaphoreType.DMA((n,))
-    nw = 6 * G if (C == 4 and R == 2) else G * (C - 1)
+    nw = 18 if (C == 4 and R == 2) else G * (C - 1)
     z, g = H - 1, G * (C - 1)
     vm = pl.BlockSpec(memory_space=pltpu.VMEM)
     hbm = pl.BlockSpec(memory_space=pl.ANY)
@@ -380,15 +415,15 @@
         in_specs=[vm, vm, vm, vm, hbm, hbm],
         out_specs=[vm, vm],
         scratch_shapes=[
-            V((T, W), BF16), V((T, W), BF16), V((8, W), F32), V((H, T, W), F32),
+            V((T, W), BF16), V((T, W), BF16), V((8, W), F32), V((H, T, W), F32), V((H, T, W), F32),
             V((G, 3, D, FG), BF16), V((H, F, W), BF16), V((H, T, W), BF16), V((H, T, W), BF16),
             V((H, 8, W), F32), V((H, T, W), BF16), V((T, HDIM), F32), V((G, 3, T, FG), BF16),
             V((T, F), F32), V((G, heads, T, T), F32), V((G, C, patches, FG), F32), V((T, F), F32),
             V((G, C, patches, FG), F32), V((G, C, patches, FG), F32), V((3, T, FG), BF16),
-            V((z, T, W), BF16), V((z, T, W), BF16), V((z, T, W), BF16), V((z, T, W), BF16),
+            V((2 * z, T, W), BF16), V((2 * z, T, W), BF16), V((2 * z, T, W), BF16), V((2 * z, T, W), BF16),
             V((T, W), F32), V((T, W), F32), V((T, HDIM), F32), V((z, T, HDIM), F32),
             dma(G + H), dma(nw), dma(nw), dma(z), dma(z), dma(z), dma(z), dma(z), dma(z),
-            dma(g), dma(g), dma(g), dma(g), dma(z), dma(z), dma(z), dma(z), dma(z), dma(z),
+            dma(g), dma(g), dma(g), dma(g), dma(2 * z), dma(2 * z), dma(2 * z), dma(2 * z), dma(z), dma(z),
         ],
         compiler_params=pltpu.CompilerParams(
             collective_id=0, has_side_effects=True, vmem_limit_bytes=50 * 1024 * 1024

time: 133 us -> 124 us (0.932)
  Pallas kernels: 127 us -> 117 us
    pallas_call x1, Pallas kernels: 127 us -> 117 us  [per_device(): pl.pallas_call(functools.partial(kernel, C, H, R, G), out_shape=[jax.Shap...]
where the time goes in v3:
time: 124 us; the launch traced here: 123 us
  Pallas kernels  117 us (94%)
  local copies, waits for them, and re-layouts  4.75 us (4%)
    pallas_call x1, Pallas kernels, per_device(): pl.pallas_call(functools.partial(kernel, C, H, R, G), out_shape=[jax.Shap...  117 us
    unnamed x8, local copies, waits for them, and re-layouts  4.06 us

profile of v3, /device:TPU:0, one launch (start us, length us, event | category | flops | bytes accessed | tf_op | source)
XLA Modules:
  0.0 122.5 jit_solution(804279725937630582)
XLA Ops:
  0.6 0.7 broadcast_in_dim.3.gain1
  1.3 0.0 copy-start
  1.3 0.9 copy-done
  2.3 0.0 copy-start.1
  2.3 0.9 copy-done.1
  3.2 0.0 copy-start.2
  3.2 0.8 copy-done.2
  4.0 117.2 %shard_map.77 = (bf16[16,8,1024]{2,1,0:T(8,128)(2,1)S(1)}, bf16[16,8,1024]{2,1,0:T(8,128)(2,1)S(1)}) custom-call(bf16[16,8,1024]{2,1,0:T(8,128)(2,1)S(1)} %copy-done, bf16[16,1024]{1,0:T(8,128)(2,1)S(1)} %copy-done.2, bf16[1,1024]{1,0:T(2,128)(2,1)S(1)} %broadcast_in_dim.3.gain1, bf16[16,8,1024]{2,1,0:T(8,128)(2,1)S(1)} %copy-done.1, ...), custom_call_target="tpu_custom_call" | custom-call | tf_op jit(solution)/shard_map/pallas_call | solution.py:412
  121.1 0.7 copy.10
  121.8 0.7 copy.11
Async XLA Ops:
  1.3 0.9 copy-start
  2.3 0.9 copy-start.1
  3.2 0.8 copy-start.2

commit v4 on v3

--- a/solution.py
+++ b/solution.py
@@ -177,10 +177,7 @@
 
     def weights(n):
         own_w[n].wait()
-        if square:
-            for j in range(3):
-                pass_on(2, j)
-        else:
+        if not square:
             for k in range(1, C):
                 ref = wall.at[n, :, pl.ds(pl.multiple_of(lax.rem(c + C - k, C) * S, S), S)]
                 i = n * (C - 1) + k - 1
@@ -206,6 +203,7 @@
     def forward(n):
         for j in range(3):
             if square:
+                pass_on(2, j)
                 for slot in (3, 4, 5):
                     took(slot, j)
             own1[:, :FG] = jnp.zeros((T, FG), F32)
@@ -283,8 +281,9 @@
         return total + mm(grads[2], wall[n, 2, rows, :], NT)
 
     if square:
-        pass_on(0, 1)
-        pass_on(1, 1)
+        for j in (1, 2):
+            pass_on(0, j)
+            pass_on(1, j)
     for cp in own_o:
         cp.wait()
     from_heads(call, cs, cr)
@@ -294,9 +293,6 @@
         gm[...] += mm(call[i], wo[i], NT)
         return carry
 
-    if square:
-        pass_on(0, 2)
-        pass_on(1, 2)
     lax.fori_loop(0, H, mixed_block, 0)
     weights(0)
     forward(0)

time: 124 us -> 125 us (level); the launches traced: 123 us -> 125 us
  Pallas kernels: 117 us -> 120 us
    pallas_call x1, Pallas kernels: 117 us -> 120 us  [per_device(): pl.pallas_call(functools.partial(kernel, C, H, R, G), out_shape=[jax.Shap...]
where the time goes in v4:
time: 125 us
  Pallas kernels  120 us (96%)
  local copies, waits for them, and re-layouts  4.75 us (4%)
    pallas_call x1, Pallas kernels, per_device(): pl.pallas_call(functools.partial(kernel, C, H, R, G), out_shape=[jax.Shap...  120 us
    unnamed x8, local copies, waits for them, and re-layouts  4.06 us

profile of v4, /device:TPU:0, one launch (start us, length us, event | category | flops | bytes accessed | tf_op | source)
XLA Modules:
  0.0 125.0 jit_solution(17470041716097576432)
XLA Ops:
  0.6 0.7 broadcast_in_dim.3.gain1
  1.3 0.0 copy-start
  1.3 0.9 copy-done
  2.3 0.0 copy-start.1
  2.3 0.9 copy-done.1
  3.2 0.0 copy-start.2
  3.2 0.8 copy-done.2
  4.0 119.6 %shard_map.77 = (bf16[16,8,1024]{2,1,0:T(8,128)(2,1)S(1)}, bf16[16,8,1024]{2,1,0:T(8,128)(2,1)S(1)}) custom-call(bf16[16,8,1024]{2,1,0:T(8,128)(2,1)S(1)} %copy-done, bf16[16,1024]{1,0:T(8,128)(2,1)S(1)} %copy-done.2, bf16[1,1024]{1,0:T(2,128)(2,1)S(1)} %broadcast_in_dim.3.gain1, bf16[16,8,1024]{2,1,0:T(8,128)(2,1)S(1)} %copy-done.1, ...), custom_call_target="tpu_custom_call" | custom-call | tf_op jit(solution)/shard_map/pallas_call | solution.py:408
  123.6 0.7 copy.10
  124.3 0.7 copy.11
Async XLA Ops:
  1.3 0.9 copy-start
  2.3 0.9 copy-start.1
  3.2 0.8 copy-start.2

commit v5 on v3

--- a/solution.py
+++ b/solution.py
@@ -354,15 +354,15 @@
     for m in range((H + 1) // 2):
         order += [H - 1 - m] + ([m] if m != H - 1 - m else [])
     mixed = own2[:, :F].astype(BF16)
-    one = (acc, s1, r1, s1s, s1r)
     two = (acc2, s2, r2, s2s, s2r)
-    for d in order:
-        acc[d] = mm(mixed, wo[d], NN)
-        chain_open(d, *one)
-    chain_step(0, *one)
+    for k in range(1, H):
+        peer = lax.rem(h + k, H)
+        s1[k - 1] = mm(mixed, wo[peer], NN).astype(BF16)
+        cp = remote(s1.at[k - 1], r1.at[k - 1], s1s.at[k - 1], s1r.at[k - 1], head=peer)
+        cp.start()
+        sent.append(cp)
+    own1[...] = mm(mixed, wo[h], NN)
     within(0)
-    for m in range(1, H - 2):
-        chain_step(m, *one)
 
     dots = jnp.zeros((T, 1), F32)
     for d in order:
@@ -370,8 +370,6 @@
         acc2[d] = part
         chain_open(d, *two)
         dots += jnp.sum(hall[d].astype(F32) * gall[d][:1, :] * part, axis=-1, keepdims=True)
-    for m in range(max(1, H - 2), H - 1):
-        chain_step(m, *one)
     corr[...] = jnp.broadcast_to(dots, corr.shape)
     for k in range(1, H):
         cp = remote(corr, rcorr.at[k - 1], ks.at[k - 1], kr.at[k - 1], head=lax.rem(h + k, H))
@@ -379,7 +377,10 @@
         sent.append(cp)
     for m in range(H - 1):
         chain_step(m, *two)
-    chain_end(*one, own1)
+    for k in range(1, H):
+        slot = r1.at[k - 1]
+        remote(slot, slot, s1s.at[k - 1], s1r.at[k - 1], head=lax.rem(h + k, H)).wait_recv()
+        own1[...] += r1[k - 1].astype(F32)
     lay_ref[...] = (hid[...].astype(F32) + own1[...]).astype(BF16).reshape(lay_ref.shape)
     for k in range(1, H):
         remote(rcorr.at[k - 1], rcorr.at[k - 1], ks.at[k - 1], kr.at[k - 1], head=lax.rem(h + k, H)).wait_recv()

time: 124 us -> 128 us (1.032)
  Pallas kernels: 117 us -> 122 us
    pallas_call x1, Pallas kernels: 117 us -> 122 us  [per_device(): pl.pallas_call(functools.partial(kernel, C, H, R, G), out_shape=[jax.Shap...]
where the time goes in v5:
time: 128 us; the launch traced here: 127 us
  Pallas kernels  122 us (95%)
  local copies, waits for them, and re-layouts  4.75 us (4%)
    pallas_call x1, Pallas kernels, per_device(): pl.pallas_call(functools.partial(kernel, C, H, R, G), out_shape=[jax.Shap...  122 us
    unnamed x8, local copies, waits for them, and re-layouts  4.06 us

profile of v5, /device:TPU:0, one launch (start us, length us, event | category | flops | bytes accessed | tf_op | source)
XLA Modules:
  0.0 127.5 jit_solution(16345723830449208147)
XLA Ops:
  0.6 0.7 broadcast_in_dim.3.gain1
  1.3 0.0 copy-start
  1.3 0.9 copy-done
  2.3 0.0 copy-start.1
  2.3 0.9 copy-done.1
  3.2 0.0 copy-start.2
  3.2 0.8 copy-done.2
  4.0 122.1 %shard_map.77 = (bf16[16,8,1024]{2,1,0:T(8,128)(2,1)S(1)}, bf16[16,8,1024]{2,1,0:T(8,128)(2,1)S(1)}) custom-call(bf16[16,8,1024]{2,1,0:T(8,128)(2,1)S(1)} %copy-done, bf16[16,1024]{1,0:T(8,128)(2,1)S(1)} %copy-done.2, bf16[1,1024]{1,0:T(2,128)(2,1)S(1)} %broadcast_in_dim.3.gain1, bf16[16,8,1024]{2,1,0:T(8,128)(2,1)S(1)} %copy-done.1, ...), custom_call_target="tpu_custom_call" | custom-call | tf_op jit(solution)/shard_map/pallas_call | solution.py:413
  126.1 0.7 copy.10
  126.8 0.7 copy.11
Async XLA Ops:
  1.3 0.9 copy-start
  2.3 0.9 copy-start.1
  3.2 0.8 copy-start.2
